TPU v7x, 32 devices: a whole 2x2x4 slice. The times are simulated.
32 devices in a mesh: groups: 2 (over y), task: 4 (over x, core), tensor: 4 (over z).
Axes of the slice: x: 2, y: 2, z: 4, core: 2. Of those that a mesh axis runs over, the one named last changes fastest.
Arguments:
- task_weight_change: bfloat16 [8, 4096, 16384], P(('groups', 'task'), None, 'tensor'), parts along dimension 0, may hold values from -90 to 90
- sketch_matrix: bfloat16 [8, 32, 16384], P(('groups', 'task'), None, 'tensor'), parts along dimension 0, may hold values from -1 to 1
Outputs:
- merged_delta: bfloat16 [8192, 16384], P(('groups', 'task'), 'tensor'), parts along dimension 0
There are 2 independent parts, one for each index of `groups`. A program takes and returns all parts, laid end to end along the dimension named above; each array names one. Nothing has to cross between parts.
All inputs are finite; a program needn't handle non-finite values.
Results may differ from a plain program's by a relative error of at most 0.007.
Values may be sent and summed in bfloat16 or wider, within the bound.
A program may use at most 128 MiB of HBM per device.

v0:
```python
import jax
import jax.numpy as jnp
from jax import lax
from jax.sharding import PartitionSpec as P

NS_ITERS = 6


def inverse_root(inner_product_matrix):
    count = inner_product_matrix.shape[0]
    identity = jnp.eye(count, dtype=jnp.float32)
    norm_scale = jnp.sqrt(jnp.sum(inner_product_matrix * inner_product_matrix))
    running_estimate = inner_product_matrix / norm_scale
    inverse = identity
    for sweep in range(NS_ITERS):
        middle = 1.5 * identity - 0.5 * jnp.dot(
            inverse, running_estimate, precision=lax.Precision.HIGHEST
        )
        running_estimate = jnp.dot(running_estimate, middle, precision=lax.Precision.HIGHEST)
        inverse = jnp.dot(middle, inverse, precision=lax.Precision.HIGHEST)
    return inverse / jnp.sqrt(norm_scale)


def self_gram(stacked):
    return jnp.einsum("trd,tsd->trs", stacked, stacked, precision=lax.Precision.HIGHEST)


def row_gram(first, second):
    return lax.dot_general(
        first, second, (((1,), (1,)), ((), ())), preferred_element_type=jnp.float32
    )


def right_total(right_stack):
    return lax.psum(row_gram(right_stack, right_stack), "tensor")


def local(task_weight_change, sketch_matrix):
    depth = task_weight_change.shape[1]
    width = task_weight_change.shape[2]
    partial_value = lax.dot_general(
        sketch_matrix,
        task_weight_change,
        (((2,), (2,)), ((0,), (0,))),
        preferred_element_type=jnp.float32,
    )
    sketch = lax.psum(partial_value, "tensor")
    lower_factor = jnp.linalg.cholesky(self_gram(sketch))
    singular_basis = jax.scipy.linalg.solve_triangular(lower_factor, sketch, lower=True).astype(
        jnp.bfloat16
    )
    right_part = jnp.einsum(
        "kov,kvp->kop", singular_basis, task_weight_change, preferred_element_type=jnp.float32
    ).astype(jnp.bfloat16)
    row_count = depth // lax.axis_size("task")
    left_all, right_all = (
        lax.all_gather(singular_basis, "task", axis=0, tiled=True),
        lax.all_gather(right_part, "task", axis=0, tiled=True),
    )
    left_stack = left_all.reshape(-1, depth)
    right_stack = right_all.reshape(-1, width)
    left_rows = lax.dynamic_slice_in_dim(
        left_stack, lax.axis_index("task") * row_count, row_count, 1
    )
    gram_left = row_gram(left_stack, left_stack)
    gram_right = right_total(right_stack)
    root_left = inverse_root(gram_left)
    root_right = inverse_root(gram_right)
    merge_scale = jnp.sqrt(jnp.diagonal(gram_right))
    core_matrix = jnp.dot(
        root_left * merge_scale[None, :], root_right.T, precision=lax.Precision.HIGHEST
    )
    mixed = jnp.dot(
        core_matrix, right_stack.astype(jnp.float32), precision=lax.Precision.HIGHEST
    ).astype(jnp.bfloat16)
    merged = lax.dot_general(
        left_rows, mixed, (((0,), (0,)), ((), ())), preferred_element_type=jnp.float32
    )
    return merged.astype(jnp.bfloat16)


def solution(mesh):
    placed = (P(("groups", "task"), None, "tensor"), P(("groups", "task"), None, "tensor"))
    return jax.shard_map(
        local,
        mesh=mesh,
        in_specs=placed,
        out_specs=P(("groups", "task"), "tensor"),
        check_vma=False,
    )
```

profile of v0, /device:TPU:0, one launch (start us, length us, event | category | flops | bytes accessed | tf_op | source)
XLA Modules:
  0.0 173.1 jit_solution(3922527049854275256)
XLA Ops:
  6.5 0.0 copy-start
  6.5 0.0 all-reduce.3.cloned.1.call-start
  6.5 0.9 copy-done
  7.5 16.0 %fusion.2 = f32[32,4096]{1,0:T(8,128)} fusion(bf16[1,4096,4096]{2,1,0:T(8,128)(2,1)} %param.2, bf16[1,32,4096]{2,1,0:T(8,128)(2,1)S(1)} %copy-done), kind=kOutput, calls=%fused_computation.3 | convolution fusion | flops 1073741824 | bytes 34340864 | tf_op jit(solution)/shard_map/dot_general | solution.py:41
  23.5 0.0 all-reduce.3.cloned.1.call-update
  23.5 0.0 all-gather.5.cloned.1.call-start
  23.6 41.1 %all-reduce.3.cloned.1.call-done = f32[32,4096]{1,0:T(8,128)} async-done(((f32[32,4096]{1,0:T(8,128)}), f32[32,4096]{1,0:T(8,128)}) %all-reduce.3.cloned.1.call-update) | async-done | bytes 524304 | tf_op jit(solution)/shard_map/psum | solution.py:47
  64.6 1.8 %fusion.29 = f32[32,32]{0,1:T(8,128)S(1)} fusion(f32[32,4096]{1,0:T(8,128)} %all-reduce.3.cloned.1.call-done), kind=kOutput, calls=%fused_computation.57 | convolution fusion | flops 50331648 | bytes 528384 | tf_op jit(solution)/shard_map/trd,tsd->trs/dot_general | solution.py:25
  66.4 0.1 copy.6
  66.5 2.9 %custom-call.8 = f32[1,32,32]{2,1,0:T(8,128)S(1)} custom-call(f32[1,32,32]{2,1,0:T(8,128)S(1)} %fusion.26), custom_call_target="Cholesky" | custom-call | tf_op jit(solution)/shard_map/jit(cholesky)/cholesky | solution.py:48
  69.4 0.6 compare_reduce_fusion
  70.1 0.7 select_select_fusion
  70.7 2.4 %custom-call.9 = f32[1,32,32]{1,2,0:T(8,128)S(1)} custom-call(f32[1,32,32]{2,1,0:T(8,128)S(1)} %select_select_fusion), custom_call_target="InvertDiagBlocksLowerTriangular" | custom-call | tf_op jit(solution)/shard_map/jit(_solve_triangular)/triangular_solve | solution.py:49
  73.2 2.4 %convolution_convert_fusion.2 = bf16[32,4096]{1,0:T(8,128)(2,1)} fusion(f32[32,4096]{1,0:T(8,128)} %all-reduce.3.cloned.1.call-done, f32[1,32,32]{1,2,0:T(8,128)S(1)} %custom-call.9), kind=kOutput, calls=%fused_computation.8 | convolution fusion | flops 50462720 | bytes 790528 | tf_op jit(solution)/shard_map/jit(_solve_triangular)/triangular_solve | solution.py:49
  75.6 0.0 all-gather.5.cloned.1.call-update
  75.6 0.0 all-gather.7.cloned.1.call-start
  75.7 17.6 %fusion.4 = bf16[32,4096]{1,0:T(8,128)(2,1)} fusion(bf16[32,4096]{1,0:T(8,128)(2,1)} %convolution_convert_fusion.2, bf16[1,4096,4096]{2,1,0:T(8,128)(2,1)} %param.2), kind=kOutput, calls=%fused_computation.7 | convolution fusion | flops 1073872896 | bytes 34078720 | tf_op jit(solution)/shard_map/kov,kvp->kop/dot_general | solution.py:52
  93.2 0.0 all-gather.7.cloned.1.call-update
  93.3 0.2 all-reduce.5.cloned.1.call-start
  93.5 0.0 all-gather.5.cloned.1.call-done
  93.5 2.6 %multiply_reduce_fusion.1 = (f32[]{:T(128)}, f32[128,128]{1,0:T(8,128)S(1)}) fusion(bf16[128,4096]{1,0:T(8,128)(2,1)} %all-gather.5.cloned.1.call-done), kind=kOutput, calls=%fused_computation.39 | convolution fusion | flops 134250496 | bytes 1114116 | tf_op jit(solution)/shard_map/dot_general | solution.py:29
  96.8 0.2 fusion.19
  97.0 0.2 fusion.24
  97.2 0.2 fusion.23
  97.4 0.2 fusion.18
  97.6 0.2 fusion.31
  97.8 0.2 fusion.30
  98.0 0.2 fusion.17
  98.3 0.2 fusion.33
  98.5 0.2 fusion.32
  98.7 0.2 fusion.16
  98.9 0.2 fusion.35
  99.1 0.2 fusion.34
  99.3 0.2 fusion.15
  99.5 0.2 fusion.36
  99.7 0.2 fusion.37
  99.9 11.0 %all-gather.7.cloned.1.call-done = bf16[128,4096]{1,0:T(8,128)(2,1)} async-done(((bf16[32,4096]{1,0:T(8,128)(2,1)}), bf16[128,4096]{1,0:T(8,128)(2,1)}) %all-gather.7.cloned.1.call-update) | async-done | bytes 1048592 | tf_op jit(solution)/shard_map/all_gather | solution.py:58
  111.0 2.7 %fusion.38 = f32[128,128]{1,0:T(8,128)} fusion(bf16[128,4096]{1,0:T(8,128)(2,1)} %all-gather.7.cloned.1.call-done), kind=kOutput, calls=%fused_computation.66 | convolution fusion | flops 134217728 | bytes 1114112 | tf_op jit(solution)/shard_map/dot_general | solution.py:29
  113.7 0.0 all-reduce.5.cloned.1.call-update
  113.7 0.2 fusion.14
  114.0 33.8 %all-reduce.5.cloned.1.call-done = f32[128,128]{1,0:T(8,128)} async-done(((f32[128,128]{1,0:T(8,128)}), f32[128,128]{1,0:T(8,128)}) %all-reduce.5.cloned.1.call-update) | async-done | bytes 65552 | tf_op jit(solution)/shard_map/psum | solution.py:35
  147.8 1.5 multiply_reduce_fusion
  150.0 1.0 fusion.12
  151.0 0.2 fusion.22
  151.2 1.0 fusion.25
  152.3 0.2 fusion.11
  152.5 0.2 fusion.40
  152.7 0.2 fusion.39
  152.9 0.2 fusion.10
  153.1 0.2 fusion.42
  153.3 0.2 fusion.41
  153.6 0.2 fusion.9
  153.8 0.2 fusion.44
  154.0 0.2 fusion.43
  154.2 0.2 fusion.8
  154.4 0.2 fusion.45
  154.6 0.2 fusion.46
  154.8 1.9 %gather_fusion = f32[128]{0:T(128)S(1)} fusion(f32[128,128]{1,0:T(8,128)} %all-reduce.5.cloned.1.call-done, s32[128]{0:T(128)S(1)} %or_bitcast_fusion), kind=kCustom, calls=%fused_computation | custom fusion | bytes 2048 | tf_op jit(solution)/shard_map/jit(diagonal)/cond/branch_0_fun/gather | solution.py:69
  156.8 0.2 fusion.7
  157.0 0.2 convolution_divide_fusion
  157.2 0.2 fusion.13
  157.4 0.3 fusion.47
  157.7 2.2 %convolution_convert_fusion.1 = bf16[128,4096]{1,0:T(8,128)(2,1)S(1)} fusion(f32[128,128]{1,0:T(8,128)S(1)} %fusion.47, bf16[128,4096]{1,0:T(8,128)(2,1)} %all-gather.7.cloned.1.call-done), kind=kOutput, calls=%fused_computation.6 | convolution fusion | flops 805830656 | bytes 2162688 | tf_op jit(solution)/shard_map/dot_general | solution.py:73
  159.9 6.7 %convolution_convert_fusion = bf16[1024,4096]{1,0:T(8,128)(2,1)} fusion(bf16[128,4096]{1,0:T(8,128)(2,1)S(1)} %convolution_convert_fusion.1, bf16[128,4096]{1,0:T(8,128)(2,1)} %all-gather.5.cloned.1.call-done, s32[]{:T(128)S(6)} %select_n.12), kind=kOutput, calls=%fused_computation.5 | convolution fusion | flops 1077936128 | bytes 9699332 | tf_op jit(solution)/shard_map/dot_general | solution.py:76
  (4 shorter events, 0.1 us)
Async XLA Ops:
  6.5 1.0 copy-start
  6.5 58.1 %all-reduce.3.cloned.1.call-start = ((), (), s32[]{:S(2)}) async-start(), calls=%async_computation | async-start | bytes 1048576 | tf_op jit(solution)/shard_map/psum | solution.py:47
  23.5 70.0 %all-gather.5.cloned.1.call-start = ((), (), s32[]{:S(2)}) async-start(), calls=%async_computation.2 | async-start | bytes 1310720 | tf_op jit(solution)/shard_map/all_gather | solution.py:57
  75.6 35.4 %all-gather.7.cloned.1.call-start = ((), (), s32[]{:S(2)}) async-start(), calls=%async_computation.3 | async-start | bytes 1310720 | tf_op jit(solution)/shard_map/all_gather | solution.py:58
  93.3 54.5 %all-reduce.5.cloned.1.call-start = ((), (), s32[]{:S(2)}) async-start(), calls=%async_computation.1 | async-start | bytes 131072 | tf_op jit(solution)/shard_map/psum | solution.py:35
Sparse Core Ops, SparseCore 0:
  23.6 40.9 all-reduce.2
  75.7 16.6 all-gather.4
  94.0 16.8 all-gather.6
  113.8 33.9 all-reduce.4
where the time goes:
time: 174 us; the launch traced here: 173 us
  waiting for transfers between devices  86 us (49%)
  matrix products  60.8 us (35%)
  between operations  14.9 us (9%)
  other arithmetic  8.16 us (5%)
  local copies, waits for them, and re-layouts  2.97 us (2%)
    psum x1, waiting for transfers between devices, local(): sketch = lax.psum(partial_value, 'tensor')  41.1 us
    psum x1, waiting for transfers between devices, right_total(): return lax.psum(row_gram(right_stack, right_stack), 'tensor')  33.8 us
    dot_general x1, matrix products, local(): jnp.einsum('kov,kvp->kop', singular_basis, task_weight_change, preferred_...  17.6 us
    dot_general x1, matrix products, local(): lax.dot_general(sketch_matrix, task_weight_change, (((2,), (2,)), ((0,),...  16 us
    all_gather x1, waiting for transfers between devices, local(): lax.all_gather(right_part, 'task', axis=0, tiled=True)  11 us
    dot_general x1, matrix products, local(): lax.dot_general(left_rows, mixed, (((0,), (0,)), ((), ())), preferred_ele...  6.72 us
    dot_general x2, matrix products, row_gram(): lax.dot_general(first, second, (((1,), (1,)), ((), ())), preferred_elemen...  5.32 us
    another operation x3, other arithmetic, local(): lower_factor = jnp.linalg.cholesky(self_gram(sketch))  3.6 us
  transfers between devices with their start and end apart: 4, of which 3 were waited for; matrix products, arithmetic and copies ran while one was open for 14% of the time, Pallas kernels for 0%

commit v1 on v0

v1 whole, which is shorter than its diff:
```python
import functools

import jax
import jax.numpy as jnp
from jax import lax
from jax.experimental import pallas as pl
from jax.experimental.pallas import tpu as pltpu
from jax.sharding import PartitionSpec as P

NS_ITERS = 6
MESH = pl.DeviceIdType.MESH
NT = (((1,), (1,)), ((), ()))
HIGHEST = lax.Precision.HIGHEST


def remote(src, dst, send, recv, axis, target):
    return pltpu.make_async_remote_copy(
        src_ref=src,
        dst_ref=dst,
        send_sem=send,
        recv_sem=recv,
        device_id={axis: target},
        device_id_type=MESH,
    )


def full(a, b):
    return jnp.dot(a, b, precision=HIGHEST, preferred_element_type=jnp.float32)


def inverse_roots(grams):
    count = grams[0].shape[0]
    row = lax.broadcasted_iota(jnp.int32, (count, count), 0)
    column = lax.broadcasted_iota(jnp.int32, (count, count), 1)
    eye = (row == column).astype(jnp.float32)
    norms, ys, zs = [], [], []
    for gram in grams:
        norm = jnp.sqrt(
            jnp.sum(jnp.sum(gram * gram, axis=1, keepdims=True), axis=0, keepdims=True)
        )
        y = gram / norm
        middle = 1.5 * eye - 0.5 * y
        norms.append(norm)
        ys.append(full(y, middle))
        zs.append(middle)
    for sweep in range(1, NS_ITERS):
        middles = [1.5 * eye - 0.5 * full(z, y) for z, y in zip(zs, ys)]
        if sweep < NS_ITERS - 1:
            ys = [full(y, middle) for y, middle in zip(ys, middles)]
        zs = [full(middle, z) for middle, z in zip(middles, zs)]
    return [z / jnp.sqrt(norm) for z, norm in zip(zs, norms)], eye


def inverse_lower(gram, rank):
    row = lax.broadcasted_iota(jnp.int32, gram.shape, 0)
    column = lax.broadcasted_iota(jnp.int32, gram.shape, 1)
    work = jnp.where(column == row + rank, 1.0, gram)
    for k in range(rank - 1):
        pivot_row = work[k : k + 1, :]
        scaled = pivot_row / work[k : k + 1, k : k + 1]
        work = work - jnp.where(row > k, work[:, k : k + 1], 0.0) * scaled
    pivots = jnp.sum(jnp.where(row == column, work, 0.0), axis=1, keepdims=True)
    return work / jnp.sqrt(pivots)


def factor_kernel(
    n, m, rows, cols,
    delta, sk, right_out, lrt_out, core_out,
    dbuf, part, rs, gp, gr, bas, sl, rst, g2, g2r, gfull, lr,
    load_sem, rs_send, rs_recv, gp_send, gp_recv, ba_send, ba_recv, sl_send, sl_recv,
    sib_send, sib_recv, chip_send, chip_recv, fwd_send, fwd_recv,
    g2_send, g2_recv, gf_send, gf_recv, lr_send, lr_recv, out_sem,
):
    j, t = lax.axis_index("tensor"), lax.axis_index("task")
    depth, width = dbuf.shape
    rank = sk.shape[1]
    ds, dt = depth // n, depth // m
    nq, nc = ds // rows, width // cols
    chips = m // 2
    chip, core = t // 2, t % 2
    sibling = t + 1 - 2 * core

    def z(i):
        return lax.rem(j + i, n)

    def x(i):
        return lax.rem(t + i, m)

    def at_row(i, q):
        return pl.multiple_of(z(i) * ds + q * rows, rows)

    def load(i, q):
        where = pl.ds(at_row(i, q), rows)
        return pltpu.make_async_copy(delta.at[0, where, :], dbuf.at[where, :], load_sem.at[i, q])

    order = list(range(1, n))
    for q in range(nq):
        for i in order:
            load(i, q).start()
    for q in range(nq):
        load(0, q).start()

    barrier = pltpu.get_barrier_semaphore()
    for i in range(1, n):
        pl.semaphore_signal(barrier, inc=1, device_id={"tensor": z(i)}, device_id_type=MESH)
    for i in range(1, m):
        pl.semaphore_signal(barrier, inc=1, device_id={"task": x(i)}, device_id_type=MESH)
    pl.semaphore_wait(barrier, n + m - 2)

    def send_part(i, q):
        return remote(
            part.at[:, pl.ds(at_row(i, q), rows)],
            rs.at[i - 1, :, pl.ds(pl.multiple_of(q * rows, rows), rows)],
            rs_send.at[i - 1, q], rs_recv.at[i - 1, q], "tensor", z(i),
        )

    def sketch(i, q):
        load(i, q).wait()
        where = pl.ds(at_row(i, q), rows)
        part[:, where] = lax.dot_general(
            sk[0], dbuf[where, :], NT, preferred_element_type=jnp.float32
        )

    def others(q, carry):
        for i in order:
            sketch(i, q)
            send_part(i, q).start()
        return carry

    def own(q, carry):
        sketch(0, q)
        return carry

    lax.fori_loop(0, nq, others, 0)
    lax.fori_loop(0, nq, own, 0)

    mine = pl.ds(pl.multiple_of(j * ds, ds), ds)
    total = part[:, mine]
    for i in order:
        for q in range(nq):
            send_part(i, q).wait_recv()
        total = total + rs[i - 1]
    gp[...] = jnp.zeros_like(gp)
    gp[:, :rank] = lax.dot_general(
        total, total, NT, precision=HIGHEST, preferred_element_type=jnp.float32
    )
    sends = [
        remote(gp, gr.at[i - 1], gp_send.at[i - 1], gp_recv.at[i - 1], "tensor", z(i))
        for i in order
    ]
    for copy in sends:
        copy.start()
    gram = gp[...]
    for i, copy in zip(order, sends):
        copy.wait_recv()
        gram = gram + gr[i - 1]
    lower = inverse_lower(gram, rank)
    blank = jnp.zeros_like(total)
    rest = [blank] * (128 // rank - 2)
    basis = full(lower, jnp.concatenate([blank, total] + rest, axis=0)).astype(jnp.bfloat16)
    bas[:, mine] = basis
    sl[t] = basis
    base = [
        remote(
            bas.at[:, mine], bas.at[:, mine], ba_send.at[i - 1], ba_recv.at[i - 1], "tensor", z(i)
        )
        for i in order
    ]
    for copy in base:
        copy.start()
    sends += base
    slices = [
        remote(sl.at[t], sl.at[t], sl_send.at[i - 1], sl_recv.at[i - 1], "task", x(i))
        for i in range(1, m)
    ]
    for copy in slices:
        copy.start()
    sends += slices
    for copy in base:
        copy.wait_recv()

    def block(c):
        return pl.ds(pl.multiple_of(c * cols, cols), cols)

    def to_sibling(c):
        here = rst.at[t, :, block(c)]
        return remote(here, here, sib_send.at[c], sib_recv.at[c], "task", sibling)

    def to_chip(i, c):
        here = rst.at[t, :, block(c)]
        target = lax.rem(chip + i, chips) * 2 + core
        return remote(here, here, chip_send.at[i - 1, c], chip_recv.at[i - 1, c], "task", target)

    def forward(i, c):
        source = lax.rem(chip + chips - i, chips) * 2 + core
        here = rst.at[source, :, block(c)]
        return remote(here, here, fwd_send.at[i - 1, c], fwd_recv.at[i - 1, c], "task", sibling)

    def compute(c):
        rst[t, :, block(c)] = jnp.dot(
            bas[...], dbuf[:, block(c)], preferred_element_type=jnp.float32
        ).astype(jnp.bfloat16)
        for i in range(1, chips):
            to_chip(i, c).start()
        to_sibling(c).start()

    def pass_on(c):
        for i in range(1, chips):
            to_chip(i, c).wait_recv()
            forward(i, c).start()

    lag = min(2, nc)

    def early(c, carry):
        compute(c)
        return carry

    def middle(c, carry):
        compute(c)
        pass_on(c - lag)
        return carry

    def late(c, carry):
        pass_on(c)
        return carry

    def collect(c, carry):
        to_sibling(c).wait_recv()
        for i in range(1, chips):
            forward(i, c).wait_recv()
        return carry

    lax.fori_loop(0, lag, early, 0)
    if nc > lag:
        lax.fori_loop(lag, nc, middle, 0)
    lefts = [
        remote(
            bas.at[:, pl.ds(pl.multiple_of(x(i) * dt, dt), dt)],
            lr.at[t], lr_send.at[i - 1], lr_recv.at[i - 1], "task", x(i),
        )
        for i in range(1, m)
    ]
    lax.fori_loop(nc - lag, nc, late, 0)
    lr[t] = bas[:, pl.ds(pl.multiple_of(t * dt, dt), dt)]
    for copy in slices:
        copy.wait_recv()
    g2[:rank, :] = lax.dot_general(
        sl[t], sl[...].reshape(m * rank, ds), NT, preferred_element_type=jnp.float32
    )
    lax.fori_loop(0, nc, collect, 0)
    stack = rst[...].reshape(m * rank, width)
    g2[rank:, :] = lax.dot_general(rst[t], stack, NT, preferred_element_type=jnp.float32)

    sums = [
        remote(g2, g2r.at[i - 1], g2_send.at[i - 1], g2_recv.at[i - 1], "tensor", z(i))
        for i in order
    ]
    for copy in sums + lefts:
        copy.start()
    sends += sums + lefts
    out_copy = pltpu.make_async_copy(rst, right_out, out_sem)
    out_copy.start()
    rows_sum = g2[...]
    for i, copy in zip(order, sums):
        copy.wait_recv()
        rows_sum = rows_sum + g2r[i - 1]
    gfull[t] = rows_sum
    gathers = [
        remote(gfull.at[t], gfull.at[t], gf_send.at[i - 1], gf_recv.at[i - 1], "task", x(i))
        for i in range(1, m)
    ]
    for copy in gathers:
        copy.start()
    sends += gathers
    for copy in lefts:
        copy.wait_recv()
    lrt_out[...] = lr[...].reshape(m * rank, dt).T
    for copy in gathers:
        copy.wait_recv()

    gram_left = gfull[:, :rank, :].reshape(m * rank, m * rank)
    gram_right = gfull[:, rank:, :].reshape(m * rank, m * rank)
    (root_left, root_right), eye = inverse_roots([gram_left, gram_right])
    strength = jnp.sqrt(jnp.sum(eye * gram_right, axis=0, keepdims=True))
    core_out[...] = lax.dot_general(
        root_left * strength, root_right, NT, precision=HIGHEST, preferred_element_type=jnp.float32
    )

    for copy in sends:
        copy.wait_send()

    def finish_part(q, carry):
        for i in order:
            send_part(i, q).wait_send()
        return carry

    def finish_right(c, carry):
        to_sibling(c).wait_send()
        for i in range(1, chips):
            to_chip(i, c).wait_send()
            forward(i, c).wait_send()
        return carry

    lax.fori_loop(0, nq, finish_part, 0)
    lax.fori_loop(0, nc, finish_right, 0)
    out_copy.wait()


def factors(n, m, delta, sk):
    _, depth, width = delta.shape
    rank = sk.shape[1]
    ds, dt, count = depth // n, depth // m, m * rank
    rows, cols = min(256, ds), min(512, width)
    nq, nc = ds // rows, width // cols
    chips = max(m // 2 - 1, 1)
    dma = pltpu.SemaphoreType.DMA
    f32, bf16 = jnp.float32, jnp.bfloat16
    vmem = pl.BlockSpec(memory_space=pltpu.VMEM)
    anywhere = pl.BlockSpec(memory_space=pl.ANY)
    return pl.pallas_call(
        functools.partial(factor_kernel, n, m, rows, cols),
        out_shape=(
            jax.ShapeDtypeStruct((m, rank, width), bf16),
            jax.ShapeDtypeStruct((dt, count), bf16),
            jax.ShapeDtypeStruct((count, count), f32),
        ),
        in_specs=[anywhere, vmem],
        out_specs=(anywhere, vmem, vmem),
        scratch_shapes=[
            pltpu.VMEM((depth, width), bf16),
            pltpu.VMEM((rank, depth), f32),
            pltpu.VMEM((n - 1, rank, ds), f32),
            pltpu.VMEM((rank, 128), f32),
            pltpu.VMEM((n - 1, rank, 128), f32),
            pltpu.VMEM((rank, depth), bf16),
            pltpu.VMEM((m, rank, ds), bf16),
            pltpu.VMEM((m, rank, width), bf16),
            pltpu.VMEM((2 * rank, count), f32),
            pltpu.VMEM((n - 1, 2 * rank, count), f32),
            pltpu.VMEM((m, 2 * rank, count), f32),
            pltpu.VMEM((m, rank, dt), bf16),
            dma((n, nq)),
            dma((n - 1, nq)),
            dma((n - 1, nq)),
            dma((n - 1,)),
            dma((n - 1,)),
            dma((n - 1,)),
            dma((n - 1,)),
            dma((m - 1,)),
            dma((m - 1,)),
            dma((nc,)),
            dma((nc,)),
            dma((chips, nc)),
            dma((chips, nc)),
            dma((chips, nc)),
            dma((chips, nc)),
            dma((n - 1,)),
            dma((n - 1,)),
            dma((m - 1,)),
            dma((m - 1,)),
            dma((m - 1,)),
            dma((m - 1,)),
            dma(()),
        ],
        compiler_params=pltpu.CompilerParams(
            collective_id=0, has_side_effects=True, vmem_limit_bytes=52 * 1024 * 1024
        ),
        name="factors",
    )(delta, sk)


def merge_kernel(lrt, core, right, out):
    high = core[...].astype(jnp.bfloat16)
    low = (core[...] - high.astype(jnp.float32)).astype(jnp.bfloat16)
    mixed = jnp.dot(high, right[...], preferred_element_type=jnp.float32) + jnp.dot(
        low, right[...], preferred_element_type=jnp.float32
    )
    out[...] = jnp.dot(
        lrt[...], mixed.astype(jnp.bfloat16), preferred_element_type=jnp.float32
    ).astype(jnp.bfloat16)


def merge(lrt, core, right):
    dt, count = lrt.shape
    width = right.shape[1]
    cols = min(512, width)
    return pl.pallas_call(
        merge_kernel,
        grid=(width // cols,),
        out_shape=jax.ShapeDtypeStruct((dt, width), jnp.bfloat16),
        in_specs=[
            pl.BlockSpec((dt, count), lambda c: (0, 0)),
            pl.BlockSpec((count, count), lambda c: (0, 0)),
            pl.BlockSpec((count, cols), lambda c: (0, c)),
        ],
        out_specs=pl.BlockSpec((dt, cols), lambda c: (0, c)),
        compiler_params=pltpu.CompilerParams(vmem_limit_bytes=32 * 1024 * 1024),
        name="merge",
    )(lrt, core, right)


def solution(mesh):
    n, m = mesh.shape["tensor"], mesh.shape["task"]

    def local(task_weight_change, sketch_matrix):
        right, lrt, core = factors(n, m, task_weight_change, sketch_matrix)
        return merge(lrt, core, right.reshape(-1, right.shape[-1]))

    placed = (P(("groups", "task"), None, "tensor"), P(("groups", "task"), None, "tensor"))
    return jax.shard_map(
        local,
        mesh=mesh,
        in_specs=placed,
        out_specs=P(("groups", "task"), "tensor"),
        check_vma=False,
    )
```

time: 174 us -> 67.3 us (0.39)
  waiting for transfers between devices: 86 us -> 0 us
  Pallas kernels: 0 us -> 66.2 us
  matrix products: 60.8 us -> 0 us
  between operations: 14.9 us -> 0.01 us
  other arithmetic: 8.16 us -> 0 us
  local copies, waits for them, and re-layouts: 2.97 us -> 0.95 us
    psum x2 -> x0, waiting for transfers between devices: 74.9 us -> none  [the longest x1 41.1 us: local(): sketch = lax.psum(partial_value, 'tensor')]
    pallas_call x0 -> x2, Pallas kernels: none -> 66.2 us  [the longest x1 59.1 us: factors(): pl.pallas_call(functools.partial(factor_kernel, n, m, rows, cols), out_sh...]
    dot_general x42 -> x0, matrix products: 58.4 us -> none  [the longest x1 17.6 us: local(): jnp.einsum('kov,kvp->kop', singular_basis, task_weight_change, preferred_...]
    all_gather x2 -> x0, waiting for transfers between devices: 11 us -> none  [the longest x1 11 us: local(): lax.all_gather(right_part, 'task', axis=0, tiled=True)]
    another operation x5 -> x0, other arithmetic: 6.68 us -> none  [the longest x3 3.6 us: local(): lower_factor = jnp.linalg.cholesky(self_gram(sketch))]
    another operation x1 -> x0, matrix products: 2.4 us -> none  [local(): jax.scipy.linalg.solve_triangular(lower_factor, sketch, lower=True)]
    gather x1 -> x0, local copies, waits for them, and re-layouts: 1.94 us -> none  [local(): merge_scale = jnp.sqrt(jnp.diagonal(gram_right))]
  transfers between devices with their start and end apart: 4 -> 0, of which waited for: 3 -> 0; matrix products, arithmetic and copies ran while one was open for 14% -> 0% of each run, Pallas kernels for 0% -> 0%
where the time goes in v1:
time: 67.3 us; the launch traced here: 67.1 us
  Pallas kernels  66.2 us (98%)
  local copies, waits for them, and re-layouts  0.95 us (1%)
    pallas_call x1, Pallas kernels, factors(): pl.pallas_call(functools.partial(factor_kernel, n, m, rows, cols), out_sh...  59.1 us
    pallas_call x1, Pallas kernels, merge(): pl.pallas_call(merge_kernel, grid=(width // cols,), out_shape=jax.ShapeDt...  7.04 us

profile of v1, /device:TPU:0, one launch (start us, length us, event | category | flops | bytes accessed | tf_op | source)
XLA Modules:
  0.0 67.1 jit_solution(15866536709613273303)
XLA Ops:
  0.0 0.0 copy-start
  0.0 0.9 %copy-done = bf16[1,32,4096]{2,1,0:T(8,128)(2,1)S(1)} copy-done((bf16[1,32,4096]{2,1,0:T(8,128)(2,1)S(1)}, bf16[1,32,4096]{2,1,0:T(8,128)(2,1)}, u32[]{:S(2)}) %copy-start) | copy-done | bytes 262168
  1.0 59.1 %factors.1 = (bf16[4,32,4096]{2,1,0:T(8,128)(2,1)S(1)}, bf16[1024,128]{1,0:T(8,128)(2,1)S(1)}, f32[128,128]{1,0:T(8,128)S(1)}) custom-call(bf16[1,4096,4096]{2,1,0:T(8,128)(2,1)} %delta.1, bf16[1,32,4096]{2,1,0:T(8,128)(2,1)S(1)} %copy-done), custom_call_target="tpu_custom_call" | custom-call | tf_op jit(solution)/shard_map/factors/pallas_call | solution.py:320
  60.1 7.0 %merge.1 = bf16[1024,4096]{1,0:T(8,128)(2,1)} custom-call(bf16[1024,128]{1,0:T(8,128)(2,1)S(1)} %get-tuple-element.8.lrt, f32[128,128]{1,0:T(8,128)S(1)} %get-tuple-element.9.core, bf16[128,4096]{1,0:T(8,128)(2,1)S(1)} %bitcast.1), custom_call_target="tpu_custom_call" | custom-call | tf_op jit(solution)/shard_map/merge/pallas_call | solution.py:387
Async XLA Ops:
  0.0 0.9 %copy-start = (bf16[1,32,4096]{2,1,0:T(8,128)(2,1)S(1)}, bf16[1,32,4096]{2,1,0:T(8,128)(2,1)}, u32[]{:S(2)}) copy-start(bf16[1,32,4096]{2,1,0:T(8,128)(2,1)} %sk.1) | copy-start | bytes 786436

commit v2 on v1

--- a/solution.py
+++ b/solution.py
@@ -66,8 +66,8 @@
 def factor_kernel(
     n, m, rows, cols,
     delta, sk, right_out, lrt_out, core_out,
-    dbuf, part, rs, gp, gr, bas, sl, rst, g2, g2r, gfull, lr,
-    load_sem, rs_send, rs_recv, gp_send, gp_recv, ba_send, ba_recv, sl_send, sl_recv,
+    skb, dbuf, part, acc, rs, gp, gr, bas, sl, rst, g2, g2r, gfull, lr,
+    sk_sem, load_sem, rs_send, rs_recv, gp_send, gp_recv, ba_send, ba_recv, sl_send, sl_recv,
     sib_send, sib_recv, chip_send, chip_recv, fwd_send, fwd_recv,
     g2_send, g2_recv, gf_send, gf_recv, lr_send, lr_recv, out_sem,
 ):
@@ -94,10 +94,15 @@
         return pltpu.make_async_copy(delta.at[0, where, :], dbuf.at[where, :], load_sem.at[i, q])
 
     order = list(range(1, n))
+    first = nq // 2
+    sk_copy = pltpu.make_async_copy(sk.at[0], skb, sk_sem)
+    sk_copy.start()
+    for q in range(first):
+        load(0, q).start()
     for q in range(nq):
         for i in order:
             load(i, q).start()
-    for q in range(nq):
+    for q in range(first, nq):
         load(0, q).start()
 
     barrier = pltpu.get_barrier_semaphore()
@@ -105,7 +110,6 @@
         pl.semaphore_signal(barrier, inc=1, device_id={"tensor": z(i)}, device_id_type=MESH)
     for i in range(1, m):
         pl.semaphore_signal(barrier, inc=1, device_id={"task": x(i)}, device_id_type=MESH)
-    pl.semaphore_wait(barrier, n + m - 2)
 
     def send_part(i, q):
         return remote(
@@ -118,7 +122,7 @@
         load(i, q).wait()
         where = pl.ds(at_row(i, q), rows)
         part[:, where] = lax.dot_general(
-            sk[0], dbuf[where, :], NT, preferred_element_type=jnp.float32
+            skb[...], dbuf[where, :], NT, preferred_element_type=jnp.float32
         )
 
     def others(q, carry):
@@ -131,8 +135,12 @@
         sketch(0, q)
         return carry
 
+    sk_copy.wait()
+    if first:
+        lax.fori_loop(0, first, own, 0)
+    pl.semaphore_wait(barrier, n + m - 2)
     lax.fori_loop(0, nq, others, 0)
-    lax.fori_loop(0, nq, own, 0)
+    lax.fori_loop(first, nq, own, 0)
 
     mine = pl.ds(pl.multiple_of(j * ds, ds), ds)
     total = part[:, mine]
@@ -176,11 +184,20 @@
     for copy in slices:
         copy.start()
     sends += slices
-    for copy in base:
-        copy.wait_recv()
 
     def block(c):
         return pl.ds(pl.multiple_of(c * cols, cols), cols)
+
+    def share(c, carry):
+        acc[:, block(c)] = jnp.dot(
+            bas[:, mine], dbuf[mine, block(c)], preferred_element_type=jnp.float32
+        )
+        return carry
+
+    lax.fori_loop(0, nc, share, 0)
+    for copy in base:
+        copy.wait_recv()
+
 
     def to_sibling(c):
         here = rst.at[t, :, block(c)]
@@ -197,9 +214,13 @@
         return remote(here, here, fwd_send.at[i - 1, c], fwd_recv.at[i - 1, c], "task", sibling)
 
     def compute(c):
-        rst[t, :, block(c)] = jnp.dot(
-            bas[...], dbuf[:, block(c)], preferred_element_type=jnp.float32
-        ).astype(jnp.bfloat16)
+        value = acc[:, block(c)]
+        for i in order:
+            where = pl.ds(pl.multiple_of(z(i) * ds, ds), ds)
+            value = value + jnp.dot(
+                bas[:, where], dbuf[where, block(c)], preferred_element_type=jnp.float32
+            )
+        rst[t, :, block(c)] = value.astype(jnp.bfloat16)
         for i in range(1, chips):
             to_chip(i, c).start()
         to_sibling(c).start()
@@ -324,11 +345,13 @@
             jax.ShapeDtypeStruct((dt, count), bf16),
             jax.ShapeDtypeStruct((count, count), f32),
         ),
-        in_specs=[anywhere, vmem],
+        in_specs=[anywhere, anywhere],
         out_specs=(anywhere, vmem, vmem),
         scratch_shapes=[
+            pltpu.VMEM((rank, width), bf16),
             pltpu.VMEM((depth, width), bf16),
             pltpu.VMEM((rank, depth), f32),
+            pltpu.VMEM((rank, width), f32),
             pltpu.VMEM((n - 1, rank, ds), f32),
             pltpu.VMEM((rank, 128), f32),
             pltpu.VMEM((n - 1, rank, 128), f32),
@@ -339,6 +362,7 @@
             pltpu.VMEM((n - 1, 2 * rank, count), f32),
             pltpu.VMEM((m, 2 * rank, count), f32),
             pltpu.VMEM((m, rank, dt), bf16),
+            dma(()),
             dma((n, nq)),
             dma((n - 1, nq)),
             dma((n - 1, nq)),
@@ -383,7 +407,7 @@
 def merge(lrt, core, right):
     dt, count = lrt.shape
     width = right.shape[1]
-    cols = min(512, width)
+    cols = min(2048, width)
     return pl.pallas_call(
         merge_kernel,
         grid=(width // cols,),

time: 67.3 us -> 65.2 us (0.969)
  Pallas kernels: 66.2 us -> 64.1 us
    pallas_call x1, Pallas kernels: 7.04 us -> 5.2 us  [merge(): pl.pallas_call(merge_kernel, grid=(width // cols,), out_shape=jax.ShapeDt...]
where the time goes in v2:
time: 65.2 us; the launch traced here: 65 us
  Pallas kernels  64.1 us (98%)
  local copies, waits for them, and re-layouts  0.95 us (1%)
    pallas_call x1, Pallas kernels, factors(): pl.pallas_call(functools.partial(factor_kernel, n, m, rows, cols), out_sh...  58.9 us
    pallas_call x1, Pallas kernels, merge(): pl.pallas_call(merge_kernel, grid=(width // cols,), out_shape=jax.ShapeDt...  5.2 us

profile of v2, /device:TPU:0, one launch (start us, length us, event | category | flops | bytes accessed | tf_op | source)
XLA Modules:
  0.0 65.0 jit_solution(18201452127969948322)
XLA Ops:
  0.0 0.0 copy-start
  0.0 0.9 %copy-done = bf16[1,32,4096]{2,1,0:T(8,128)(2,1)S(1)} copy-done((bf16[1,32,4096]{2,1,0:T(8,128)(2,1)S(1)}, bf16[1,32,4096]{2,1,0:T(8,128)(2,1)}, u32[]{:S(2)}) %copy-start) | copy-done | bytes 262168
  1.0 58.9 %factors.1 = (bf16[4,32,4096]{2,1,0:T(8,128)(2,1)S(1)}, bf16[1024,128]{1,0:T(8,128)(2,1)S(1)}, f32[128,128]{1,0:T(8,128)S(1)}) custom-call(bf16[1,4096,4096]{2,1,0:T(8,128)(2,1)} %delta.1, bf16[1,32,4096]{2,1,0:T(8,128)(2,1)S(1)} %copy-done), custom_call_target="tpu_custom_call" | custom-call | tf_op jit(solution)/shard_map/factors/pallas_call | solution.py:341
  59.8 5.2 %merge.1 = bf16[1024,4096]{1,0:T(8,128)(2,1)} custom-call(bf16[1024,128]{1,0:T(8,128)(2,1)S(1)} %get-tuple-element.8.lrt, f32[128,128]{1,0:T(8,128)S(1)} %get-tuple-element.9.core, bf16[128,4096]{1,0:T(8,128)(2,1)S(1)} %bitcast.1), custom_call_target="tpu_custom_call" | custom-call | tf_op jit(solution)/shard_map/merge/pallas_call | solution.py:411
Async XLA Ops:
  0.0 0.9 %copy-start = (bf16[1,32,4096]{2,1,0:T(8,128)(2,1)S(1)}, bf16[1,32,4096]{2,1,0:T(8,128)(2,1)}, u32[]{:S(2)}) copy-start(bf16[1,32,4096]{2,1,0:T(8,128)(2,1)} %sk.1) | copy-start | bytes 786436
